TPU v7x, 256 devices: a whole 4x4x8 slice. The times are simulated.
256 devices in a mesh: node: 64 (over x, z_hi, y, core), local: 4 (over z_lo).
Axes of the slice: x: 4, y: 4, z: 8 (z_hi: 2, z_lo: 4; z = z_hi * 4 + z_lo), core: 2. Of those that a mesh axis runs over, the one named last changes fastest.
Arguments:
- tokens: bfloat16 [32768, 4096], P(('node', 'local')), may hold values from -24 to 24
- cotangent: bfloat16 [32768, 4096], P(('node', 'local')), may hold values from -0.03125 to 0.03125
- master: float32 [4096, 4096], P('node', 'local'), may hold values from -3 to 3
- moment: float32 [4096, 4096], P('node', 'local'), may hold values from -5 to 5
- second: float32 [4096, 4096], P('node', 'local'), may hold values from 0.1 to 2
Outputs:
- master_new: float32 [4096, 4096], P('node', 'local')
- moment_new: float32 [4096, 4096], P('node', 'local')
- second_new: float32 [4096, 4096], P('node', 'local')
- weights: bfloat16 [4096, 4096], P(None, 'local')
All inputs are finite; a program needn't handle non-finite values.
Results may differ from a plain program's by a relative error of at most 0.001.
Values may be sent and summed in bfloat16 or wider, within the bound.
A program may use at most 192 MiB of HBM per device.

v0:
```python
import jax
import jax.numpy as jnp
from jax import lax
from jax.sharding import PartitionSpec as P

first_beta = 0.9
second_beta = 0.95
learn_rate = 0.01
decay_rate = 0.1
epsilon = 1e-08
first_fix = 1.0 - 0.9**20
second_fix = 1.0 - 0.95**20


def contract_tokens(left, right):
    return lax.dot_general(
        left, right, (((0,), (0,)), ((), ())), preferred_element_type=jnp.float32
    )


def on_device(tokens, cotangent, master, moment, second):
    gathered_tokens = lax.all_gather(tokens, "local", axis=0, tiled=True)
    column_cotangent = lax.all_to_all(cotangent, "local", split_axis=1, concat_axis=0, tiled=True)
    gradient = lax.psum_scatter(
        contract_tokens(gathered_tokens, column_cotangent), "node", scatter_dimension=0, tiled=True
    )
    moment_new = first_beta * moment + (1.0 - first_beta) * gradient
    second_new = second_beta * second + (1.0 - second_beta) * gradient * gradient
    update = (
        moment_new / first_fix / (jnp.sqrt(second_new / second_fix) + epsilon) + decay_rate * master
    )
    master_new = master - learn_rate * update
    weights = lax.all_gather(master_new.astype(jnp.bfloat16), "node", axis=0, tiled=True)
    return (master_new, moment_new, second_new, weights)


def solution(mesh):
    placed = (
        P(("node", "local"), None),
        P(("node", "local"), None),
        P("node", "local"),
        P("node", "local"),
        P("node", "local"),
    )
    return jax.shard_map(
        on_device,
        mesh=mesh,
        in_specs=placed,
        out_specs=(P("node", "local"), P("node", "local"), P("node", "local"), P(None, "local")),
        check_vma=False,
    )
```

profile of v0, /device:TPU:1, one launch (start us, length us, event | category | flops | bytes accessed | tf_op | source)
XLA Modules:
  0.0 694.8 jit_solution(13387764995436822518)
XLA Ops:
  7.2 0.0 all-gather.3.cloned.1.call-start
  7.2 0.7 all-gather.3.cloned.1.call-update
  7.9 0.0 reduce-scatter.2.cloned.1.call-start
  7.9 1.6 copy.9
  9.6 48.0 %all_to_all.19 = bf16[128,4,1024]{0,2,1:T(8,128)(2,1)S(1)} all-to-all(bf16[128,4,1024]{0,2,1:T(8,128)(2,1)S(1)} %bitcast.6), channel_id=1, replica_groups=mesh['node'=64,'local'=4] {'local'}, dimensions={1} | all-to-all | bytes 2097152 | tf_op jit(solution)/shard_map/all_to_all | solution.py:23
  57.5 0.5 copy.10
  58.1 45.6 %all-gather.3.cloned.1.call-done = bf16[512,4096]{1,0:T(8,128)(2,1)} async-done(((bf16[128,4096]{1,0:T(8,128)(2,1)}), bf16[512,4096]{1,0:T(8,128)(2,1)}) %all-gather.3.cloned.1.call-update) | async-done | bytes 4194320 | tf_op jit(solution)/shard_map/all_gather | solution.py:22
  103.7 10.3 %fusion.3 = f32[4096,1024]{1,0:T(8,128)} fusion(bf16[512,4096]{1,0:T(8,128)(2,1)} %all-gather.3.cloned.1.call-done, bf16[512,1024]{1,0:T(8,128)(2,1)S(1)} %bitcast.7), kind=kOutput, calls=%fused_computation.5 | convolution fusion | flops 4294967296 | bytes 22020096 | tf_op jit(solution)/shard_map/dot_general | solution.py:16
  114.0 0.0 copy-start
  114.0 0.0 copy-start.1
  114.0 0.0 copy-start.2
  114.0 0.0 reduce-scatter.2.cloned.1.call-update
  114.1 0.0 all-gather.5.cloned.1.call-start
  114.1 444.9 %reduce-scatter.2.cloned.1.call-done = f32[64,1024]{1,0:T(8,128)} async-done(((f32[4096,1024]{1,0:T(8,128)}), f32[64,1024]{1,0:T(8,128)}) %reduce-scatter.2.cloned.1.call-update) | async-done | bytes 262160 | tf_op jit(solution)/shard_map/reduce_scatter | solution.py:24
  559.0 0.0 copy-done
  559.0 0.0 copy-done.1
  559.0 0.0 copy-done.2
  559.0 2.0 fusion.1
  561.0 0.0 all-gather.5.cloned.1.call-update
  561.0 119.4 %all-gather.5.cloned.1.call-done = bf16[4096,1024]{1,0:T(8,128)(2,1)} async-done(((bf16[64,1024]{1,0:T(8,128)(2,1)}), bf16[4096,1024]{1,0:T(8,128)(2,1)}) %all-gather.5.cloned.1.call-update) | async-done | bytes 8388624 | tf_op jit(solution)/shard_map/all_gather | solution.py:33
  680.5 7.8 %copy.12 = bf16[4096,1024]{1,0:T(8,128)(2,1)} copy(bf16[4096,1024]{1,0:T(8,128)(2,1)} %all-gather.5.cloned.1.call-done) | data formatting | bytes 16777216
Async XLA Ops:
  7.2 96.5 %all-gather.3.cloned.1.call-start = ((), (), s32[]{:S(2)}) async-start(), calls=%async_computation.2 | async-start | bytes 5242880 | tf_op jit(solution)/shard_map/all_gather | solution.py:22
  7.9 551.1 %reduce-scatter.2.cloned.1.call-start = ((), (), s32[]{:S(2)}) async-start(), calls=%async_computation.3 | async-start | bytes 17039360 | tf_op jit(solution)/shard_map/reduce_scatter | solution.py:24
  114.0 445.0 %copy-start = (f32[64,1024]{1,0:T(8,128)S(1)}, f32[64,1024]{1,0:T(8,128)}, u32[]{:S(2)}) copy-start(f32[64,1024]{1,0:T(8,128)} %param.7) | copy-start | bytes 786436
  114.0 445.0 %copy-start.1 = (f32[64,1024]{1,0:T(8,128)S(1)}, f32[64,1024]{1,0:T(8,128)}, u32[]{:S(2)}) copy-start(f32[64,1024]{1,0:T(8,128)} %param.8) | copy-start | bytes 786436
  114.0 445.0 %copy-start.2 = (f32[64,1024]{1,0:T(8,128)S(1)}, f32[64,1024]{1,0:T(8,128)}, u32[]{:S(2)}) copy-start(f32[64,1024]{1,0:T(8,128)} %param.9) | copy-start | bytes 786436
  114.1 566.4 %all-gather.5.cloned.1.call-start = ((), (), s32[]{:S(2)}) async-start(), calls=%async_computation.4 | async-start | bytes 8519680 | tf_op jit(solution)/shard_map/all_gather | solution.py:33
Sparse Core Ops, SparseCore 0:
  9.8 93.8 all-gather.2
  114.2 444.7 reduce-scatter.1
  563.2 117.2 all-gather.4
where the time goes:
time: 695 us
  waiting for transfers between devices  611 us (88%)
  blocking collectives  48 us (7%)
  between operations  13.8 us (2%)
  matrix products  10.3 us (1%)
  local copies, waits for them, and re-layouts  9.91 us (1%)
    reduce_scatter x1, waiting for transfers between devices, on_device(): lax.psum_scatter(contract_tokens(gathered_tokens, column_cotangent), 'nod...  445 us
    all_gather x1, waiting for transfers between devices, on_device(): lax.all_gather(master_new.astype(jnp.bfloat16), 'node', axis=0, tiled=True)  119 us
    all_to_all x1, blocking collectives, on_device(): lax.all_to_all(cotangent, 'local', split_axis=1, concat_axis=0, tiled=True)  48 us
    all_gather x1, waiting for transfers between devices, on_device(): gathered_tokens = lax.all_gather(tokens, 'local', axis=0, tiled=True)  45.6 us
  transfers between devices with their start and end apart: 3, of which 3 were waited for; matrix products, arithmetic and copies ran while one was open for 0% of the time, Pallas kernels for 0%

commit v1 on v0

v1 whole, which is shorter than its diff:
```python
import jax
import jax.numpy as jnp
from jax import lax
from jax.experimental import pallas as pl
from jax.experimental.pallas import tpu as pltpu
from jax.sharding import PartitionSpec as P

MESH = pl.DeviceIdType.MESH

first_beta = 0.9
second_beta = 0.95
learn_rate = 0.01
decay_rate = 0.1
epsilon = 1e-08
first_fix = 1.0 - 0.9**20
second_fix = 1.0 - 0.95**20

SLICES = 4
SR = 64 // SLICES


def kernel(
    tok, cot, master, moment, second,
    master_new, moment_new, second_new, weights,
    tg, cg, part, core_in, z_in, grad, shard, ssem, rsem, lsem,
):
    node, l = lax.axis_index("node"), lax.axis_index("local")
    c = node % 2
    y = (node // 2) % 4
    h = (node // 8) % 2
    x = node // 16
    z = h * 4 + l

    def dev(dx=0, dy=0, dz=0, dc=0):
        zz = (z + dz + 8) % 8
        xx, yy, cc = (x + dx + 4) % 4, (y + dy + 4) % 4, (c + dc) % 2
        return (((xx * 2 + zz // 4) * 4 + yy) * 2 + cc, zz % 4)

    count = [0]

    def ids(n=1):
        first = count[0]
        count[0] += n
        return first

    def rcopy(src, dst, sid, to):
        return pltpu.make_async_remote_copy(
            src_ref=src, dst_ref=dst, send_sem=ssem.at[sid], recv_sem=rsem.at[sid],
            device_id=to, device_id_type=MESH,
        )

    sent = []

    def start(cp):
        cp.start()
        sent.append(cp)

    barrier = pltpu.get_barrier_semaphore()
    peers = [dev(dx=d) for d in (1, 2, 3)] + [dev(dy=d) for d in (1, 2, 3)]
    peers += [dev(dz=1), dev(dz=-1), dev(dz=4), dev(dc=1)]
    for p in peers:
        pl.semaphore_signal(barrier, inc=1, device_id=p, device_id_type=MESH)
    pl.semaphore_wait(barrier, len(peers))

    def cols(b):
        return pl.ds(pl.multiple_of(b * 1024, 1024), 1024)

    def slot(buf, ry, rx, lo=0, n=128):
        return buf.at[ry, pl.ds(rx * 128 + lo, n)]

    own_t, own_c = tok.at[:, cols(x)], cot.at[:, cols(y)]
    lt = pltpu.make_async_copy(own_t, slot(tg, 0, 0), lsem.at[0])
    lc = pltpu.make_async_copy(own_c, slot(cg, 0, 0), lsem.at[1])
    lt.start()
    lc.start()
    ta, ca = {}, {}
    for d in (1, 3, 2):
        r = (4 - d) % 4
        ta[r] = rcopy(tok.at[:, cols((x + d) % 4)], slot(tg, 0, r), ids(), dev(dx=d))
        ca[r] = rcopy(cot.at[:, cols((y + d) % 4)], slot(cg, r, 0), ids(), dev(dy=d))
        start(ta[r])
        start(ca[r])
    tp, tm, cp_, cm = {}, {}, {}, {}

    def spread_t(rx):
        src = own_t if rx == 0 else slot(tg, 0, rx)
        tp[rx] = rcopy(src, slot(tg, 3, rx), ids(), dev(dy=1))
        tm[rx] = rcopy(src, slot(tg, 1, rx), ids(), dev(dy=-1))
        start(tp[rx])
        start(tm[rx])

    def spread_c(ry):
        src = own_c if ry == 0 else slot(cg, ry, 0)
        cp_[ry] = rcopy(src, slot(cg, ry, 3), ids(), dev(dx=1))
        cm[ry] = rcopy(src, slot(cg, ry, 1), ids(), dev(dx=-1))
        start(cp_[ry])
        start(cm[ry])

    spread_t(0)
    spread_c(0)
    for r in (3, 1, 2):
        ta[r].wait_recv()
        spread_t(r)
        ca[r].wait_recv()
        spread_c(r)
    tfp, tfm, cfp, cfm = {}, {}, {}, {}
    lt.wait()
    lc.wait()

    def forward(r):
        tp[r].wait_recv()
        tfp[r] = rcopy(slot(tg, 3, r, 0, 64), slot(tg, 2, r, 0, 64), ids(), dev(dy=1))
        start(tfp[r])
        cp_[r].wait_recv()
        cfp[r] = rcopy(slot(cg, r, 3, 0, 64), slot(cg, r, 2, 0, 64), ids(), dev(dx=1))
        start(cfp[r])
        tm[r].wait_recv()
        tfm[r] = rcopy(slot(tg, 1, r, 64, 64), slot(tg, 2, r, 64, 64), ids(), dev(dy=-1))
        start(tfm[r])
        cm[r].wait_recv()
        cfm[r] = rcopy(slot(cg, r, 1, 64, 64), slot(cg, r, 2, 64, 64), ids(), dev(dx=-1))
        start(cfm[r])

    def tile(ry, m, first):
        rows = pl.ds(pl.multiple_of(m * 256, 256), 256)
        for n in range(2):
            out = pl.ds(n * 512, 512)
            got = lax.dot_general(
                tg[ry, :, rows], cg[ry, :, out], (((0,), (0,)), ((), ())),
                preferred_element_type=jnp.float32,
            )
            part[rows, out] = got if first else part[rows, out] + got

    def matmul(ry, first):
        @pl.loop(0, 4)
        def _(m):
            tile(ry, m, first)

    forward(0)
    forward(3)
    cfp[0].wait_recv()
    cfm[0].wait_recv()
    matmul(0, True)
    forward(1)
    cfp[3].wait_recv()
    cfm[3].wait_recv()
    forward(2)
    matmul(3, False)
    cfp[1].wait_recv()
    cfm[1].wait_recv()
    matmul(1, False)
    cfp[2].wait_recv()
    cfm[2].wait_recv()
    for r in range(4):
        tfp[r].wait_recv()
        tfm[r].wait_recv()

    core_id = ids(8)

    def block(hh, yy, cc, lo=0, n=64):
        return pl.ds(pl.multiple_of(hh * 512 + yy * 128 + cc * 64 + lo, n), n)

    def core_copy(hh, yy):
        return rcopy(
            part.at[block(hh, yy, 1 - c)], core_in.at[hh, yy], core_id + hh * 4 + yy, dev(dc=1)
        )

    for m in range(4):
        tile(2, m, False)
        for b in (2 * m, 2 * m + 1):
            start(core_copy(b // 4, b % 4))

    r = (z - y + 8) % 8
    q = r % 4
    end = q == 0
    z_id = [ids(4 * SLICES), ids(4 * SLICES)]
    g_id = ids(4 * SLICES)

    def z_copy(way, hh, s, yy):
        return rcopy(
            part.at[block(hh, yy, c, s * SR, SR)], z_in.at[way, s, yy],
            z_id[way] + s * 4 + yy, dev(dz=1 - 2 * way),
        )

    def g_copy(s, yy):
        return pltpu.make_async_remote_copy(
            src_ref=part.at[block(h, yy, c, s * SR, SR)], dst_ref=grad.at[s],
            send_sem=ssem.at[g_id + s * 4 + yy], recv_sem=rsem.at[g_id + s],
            device_id=(((x * 2 + h) * 4 + yy) * 2 + c, l), device_id_type=MESH,
        )

    def core_sum(hh, yy):
        core_copy(hh, yy).wait_recv()
        part[block(hh, yy, c)] += core_in[hh, yy]

    order = ((2, 3, 0, 1), (0, 1, 2, 3))

    @pl.when(jnp.logical_not(end))
    def _():
        up = jnp.where(r < 4, 1, 0)
        for s in range(SLICES):
            for i in range(4):
                for way in range(2):
                    hh = up if way == 0 else 1 - up
                    yy = order[way][i]
                    if s == 0:
                        core_sum(hh, yy)

                    def add():
                        z_copy(way, hh, s, yy).wait_recv()
                        rows = block(hh, yy, c, s * SR, SR)
                        part[rows] += z_in[way, s, yy]

                    if i < 2:
                        pl.when(q != (1 if way == 0 else 3))(add)
                    else:
                        add()
                    z_copy(way, hh, s, yy).start()

    @pl.when(end)
    def _():
        for i in range(2):
            for way in range(2):
                core_sum(1 - h, order[way][i + 2])
        for s in range(SLICES):
            for i in range(2):
                for way in range(2):
                    z_copy(way, 1 - h, s, order[way][i + 2]).start()
        for yy in range(4):
            core_sum(h, yy)
        for s in range(SLICES):
            for yy in range(4):
                z_copy(0, h, s, yy).wait_recv()
                z_copy(1, h, s, yy).wait_recv()
                rows = block(h, yy, c, s * SR, SR)
                total = part[rows] + (z_in[0, s, yy] + z_in[1, s, yy])
                part[rows] = total

                @pl.when(yy == y)
                def _():
                    grad[s] = total

                @pl.when(yy != y)
                def _():
                    g_copy(s, yy).start()

    for s in range(SLICES):
        @pl.when(jnp.logical_not(end))
        def _():
            g_copy(s, 0).wait_recv()

        rows = pl.ds(s * SR, SR)
        g = grad[s]
        m_new = first_beta * moment[rows] + (1.0 - first_beta) * g
        s_new = second_beta * second[rows] + (1.0 - second_beta) * g * g
        old = master[rows]
        update = m_new / first_fix / (jnp.sqrt(s_new / second_fix) + epsilon) + decay_rate * old
        new = old - learn_rate * update
        master_new[rows] = new
        moment_new[rows] = m_new
        second_new[rows] = s_new
        shard[rows] = new.astype(jnp.bfloat16)

    def da(d):
        return dev(dx=d * (1 - c), dy=d * c)

    def db(d):
        return dev(dx=d * c, dy=d * (1 - c))

    def unit(hh, a=0, b=0):
        xx = (x + a * (1 - c) + b * c + 4) % 4
        yy = (y + a * c + b * (1 - c) + 4) % 4
        return weights.at[xx, hh, yy, c]

    both = slice(None)
    side = dev(dc=1)
    own = pltpu.make_async_copy(shard, unit(h), lsem.at[2])
    own.start()
    w_z = rcopy(shard, unit(h), ids(), dev(dz=4))
    w_a = {(0, 1): rcopy(shard, unit(h), ids(), da(1)), (0, -1): rcopy(shard, unit(h), ids(), da(-1))}
    start(w_z)
    start(w_a[0, 1])
    start(w_a[0, -1])
    sib = []

    def to_side(hh, a=0, b=0):
        cp = rcopy(unit(hh, a, b), unit(hh, a, b), ids(), side)
        start(cp)
        sib.append(cp)

    own.wait()
    to_side(h)
    w_z.wait_recv()
    for d in (1, -1):
        w_a[1, d] = rcopy(unit(1 - h), unit(1 - h), ids(), da(d))
        start(w_a[1, d])
    to_side(1 - h)
    w_b = {}

    def b_send(a):
        for d in (1, -1):
            w_b[a, d] = rcopy(unit(both, a), unit(both, a), ids(), db(d))
            start(w_b[a, d])

    b_send(0)
    f_a = {}
    w_a[0, 1].wait_recv()
    f_a[1] = rcopy(unit(h, -1), unit(h, -1), ids(), da(1))
    start(f_a[1])
    w_a[1, -1].wait_recv()
    f_a[-1] = rcopy(unit(1 - h, 1), unit(1 - h, 1), ids(), da(-1))
    start(f_a[-1])
    w_a[1, 1].wait_recv()
    b_send(-1)
    w_a[0, -1].wait_recv()
    b_send(1)
    to_side(both, -1)
    to_side(both, 1)
    f_a[1].wait_recv()
    f_a[-1].wait_recv()
    b_send(2)
    to_side(both, 2)
    f_b = {}
    for a in (0, -1, 1, 2):
        w_b[a, 1].wait_recv()
        f_b[a, 1] = rcopy(unit(0, a, -1), unit(0, a, -1), ids(), db(1))
        start(f_b[a, 1])
        w_b[a, -1].wait_recv()
        f_b[a, -1] = rcopy(unit(1, a, 1), unit(1, a, 1), ids(), db(-1))
        start(f_b[a, -1])
        to_side(both, a, -1)
        to_side(both, a, 1)
    for a in (0, -1, 1, 2):
        f_b[a, 1].wait_recv()
        f_b[a, -1].wait_recv()
        to_side(both, a, 2)
    for cp in sib:
        cp.wait_recv()
    for cp in sent:
        cp.wait_send()

    @pl.when(jnp.logical_not(end))
    def _():
        for s in range(SLICES):
            for yy in range(4):
                for way in range(2):
                    z_copy(way, 0, s, yy).wait_send()

    @pl.when(end)
    def _():
        for s in range(SLICES):
            for i in range(2):
                for way in range(2):
                    z_copy(way, 1 - h, s, order[way][i + 2]).wait_send()
            for yy in range(4):
                @pl.when(yy != y)
                def _():
                    g_copy(s, yy).wait_send()


N_SEM = 256


def on_device(tokens, cotangent, master, moment, second):
    vmem, hbm = pl.BlockSpec(memory_space=pltpu.VMEM), pl.BlockSpec(memory_space=pl.ANY)
    f32 = jax.ShapeDtypeStruct((64, 1024), jnp.float32)
    out = pl.pallas_call(
        kernel,
        out_shape=(f32, f32, f32, jax.ShapeDtypeStruct((4, 2, 4, 2, 64, 1024), jnp.bfloat16)),
        in_specs=[hbm, hbm, vmem, vmem, vmem],
        out_specs=(vmem, vmem, vmem, hbm),
        scratch_shapes=[
            pltpu.VMEM((4, 512, 1024), jnp.bfloat16),
            pltpu.VMEM((4, 512, 1024), jnp.bfloat16),
            pltpu.VMEM((1024, 1024), jnp.float32),
            pltpu.VMEM((2, 4, 64, 1024), jnp.float32),
            pltpu.VMEM((2, SLICES, 4, SR, 1024), jnp.float32),
            pltpu.VMEM((SLICES, SR, 1024), jnp.float32),
            pltpu.VMEM((64, 1024), jnp.bfloat16),
            pltpu.SemaphoreType.DMA((N_SEM,)),
            pltpu.SemaphoreType.DMA((N_SEM,)),
            pltpu.SemaphoreType.DMA((3,)),
        ],
        compiler_params=pltpu.CompilerParams(
            collective_id=0, has_side_effects=True, vmem_limit_bytes=48 * 2**20
        ),
    )(tokens, cotangent, master, moment, second)
    return (*out[:3], out[3].reshape(4096, 1024))


def solution(mesh):
    placed = (
        P(("node", "local"), None),
        P(("node", "local"), None),
        P("node", "local"),
        P("node", "local"),
        P("node", "local"),
    )
    return jax.shard_map(
        on_device,
        mesh=mesh,
        in_specs=placed,
        out_specs=(P("node", "local"), P("node", "local"), P("node", "local"), P(None, "local")),
        check_vma=False,
    )
```

time: 695 us -> 349 us (0.50)
  the two profiles are of different devices: /device:TPU:1 before, /device:TPU:33 now
where the time goes in v1:
time: 349 us; the launch traced here: 348 us
  Pallas kernels  332 us (95%)
  local copies, waits for them, and re-layouts  15.2 us (4%)
    pallas_call x1, Pallas kernels, on_device(): pl.pallas_call(kernel, out_shape=(f32, f32, f32, jax.ShapeDtypeStruct((4,...  332 us
    unnamed x14, local copies, waits for them, and re-layouts  15.2 us

profile of v1, /device:TPU:33, one launch (start us, length us, event | category | flops | bytes accessed | tf_op | source)
XLA Modules:
  0.0 348.3 jit_solution(14278939940457453631)
XLA Ops:
  0.6 0.0 copy-start
  0.6 1.2 copy-done
  1.9 0.0 copy-start.1
  1.9 1.2 copy-done.1
  3.1 0.0 copy-start.2
  3.1 0.9 copy-done.2
  4.0 0.0 copy-start.3
  4.0 0.9 copy-done.3
  5.0 0.0 copy-start.4
  5.0 0.9 copy-done.4
  5.9 332.5 %shard_map.84 = (f32[64,1024]{1,0:T(8,128)S(1)}, f32[64,1024]{1,0:T(8,128)S(1)}, f32[64,1024]{1,0:T(8,128)S(1)}, bf16[4,2,4,2,64,1024]{5,4,3,2,1,0:T(8,128)(2,1)}) custom-call(bf16[128,4096]{1,0:T(8,128)(2,1)S(1)} %copy-done, bf16[128,4096]{1,0:T(8,128)(2,1)S(1)} %copy-done.1, f32[64,1024]{1,0:T(8,128)S(1)} %copy-done.2, f32[64,1024]{1,0:T(8,128)S(1)} %copy-done.3, ...), custom_call_target="tpu_custom_call" | custom-call | tf_op jit(solution)/shard_map/pallas_call | solution.py:367
  338.4 0.7 copy.13
  339.1 0.7 copy.14
  339.8 0.7 copy.15
  340.5 7.8 %copy.16 = bf16[4096,1024]{1,0:T(8,128)(2,1)} copy(bf16[4096,1024]{1,0:T(8,128)(2,1)} %bitcast.1) | data formatting | bytes 16777216
Async XLA Ops:
  0.6 1.2 copy-start
  1.9 1.2 copy-start.1
  3.1 0.9 copy-start.2
  4.0 0.9 copy-start.3
  5.0 0.9 copy-start.4

commit v2 on v1

--- a/solution.py
+++ b/solution.py
@@ -15,6 +15,7 @@
 first_fix = 1.0 - 0.9**20
 second_fix = 1.0 - 0.95**20
 
+LAG = 2
 SLICES = 4
 SR = 64 // SLICES
 
@@ -195,27 +196,23 @@
 
     order = ((2, 3, 0, 1), (0, 1, 2, 3))
 
-    @pl.when(jnp.logical_not(end))
-    def _():
-        up = jnp.where(r < 4, 1, 0)
-        for s in range(SLICES):
-            for i in range(4):
-                for way in range(2):
-                    hh = up if way == 0 else 1 - up
-                    yy = order[way][i]
-                    if s == 0:
-                        core_sum(hh, yy)
-
-                    def add():
-                        z_copy(way, hh, s, yy).wait_recv()
-                        rows = block(hh, yy, c, s * SR, SR)
-                        part[rows] += z_in[way, s, yy]
-
-                    if i < 2:
-                        pl.when(q != (1 if way == 0 else 3))(add)
-                    else:
-                        add()
-                    z_copy(way, hh, s, yy).start()
+    up = jnp.where(r < 4, 1, 0)
+    for place in (1, 2, 3):
+        steps = [(k + LAG * (place - 1 if way == 0 else 3 - place), way, k) for k in range(4 * SLICES) for way in range(2)]
+
+        @pl.when(q == place)
+        def _():
+            for _, way, k in sorted(steps):
+                hh = up if way == 0 else 1 - up
+                s, i = k // 4, k % 4
+                yy = order[way][i]
+                if s == 0:
+                    core_sum(hh, yy)
+                if i >= 2 or place != (1 if way == 0 else 3):
+                    z_copy(way, hh, s, yy).wait_recv()
+                    rows = block(hh, yy, c, s * SR, SR)
+                    part[rows] += z_in[way, s, yy]
+                z_copy(way, hh, s, yy).start()
 
     @pl.when(end)
     def _():

time: 349 us -> 153 us (0.44)
  the two profiles are of different devices: /device:TPU:33 before, /device:TPU:1 now
where the time goes in v2:
time: 153 us
  Pallas kernels  137 us (90%)
  local copies, waits for them, and re-layouts  15.2 us (10%)
    pallas_call x1, Pallas kernels, on_device(): pl.pallas_call(kernel, out_shape=(f32, f32, f32, jax.ShapeDtypeStruct((4,...  137 us
    unnamed x14, local copies, waits for them, and re-layouts  15.2 us

profile of v2, /device:TPU:1, one launch (start us, length us, event | category | flops | bytes accessed | tf_op | source)
XLA Modules:
  0.0 153.2 jit_solution(1903672283874224340)
XLA Ops:
  0.6 0.0 copy-start
  0.6 1.2 copy-done
  1.9 0.0 copy-start.1
  1.9 1.2 copy-done.1
  3.1 0.0 copy-start.2
  3.1 0.9 copy-done.2
  4.0 0.0 copy-start.3
  4.0 0.9 copy-done.3
  5.0 0.0 copy-start.4
  5.0 0.9 copy-done.4
  5.9 137.4 %shard_map.84 = (f32[64,1024]{1,0:T(8,128)S(1)}, f32[64,1024]{1,0:T(8,128)S(1)}, f32[64,1024]{1,0:T(8,128)S(1)}, bf16[4,2,4,2,64,1024]{5,4,3,2,1,0:T(8,128)(2,1)}) custom-call(bf16[128,4096]{1,0:T(8,128)(2,1)S(1)} %copy-done, bf16[128,4096]{1,0:T(8,128)(2,1)S(1)} %copy-done.1, f32[64,1024]{1,0:T(8,128)S(1)} %copy-done.2, f32[64,1024]{1,0:T(8,128)S(1)} %copy-done.3, ...), custom_call_target="tpu_custom_call" | custom-call | tf_op jit(solution)/shard_map/pallas_call | solution.py:364
  143.3 0.7 copy.13
  144.0 0.7 copy.14
  144.7 0.7 copy.15
  145.4 7.8 %copy.16 = bf16[4096,1024]{1,0:T(8,128)(2,1)} copy(bf16[4096,1024]{1,0:T(8,128)(2,1)} %bitcast.1) | data formatting | bytes 16777216
Async XLA Ops:
  0.6 1.2 copy-start
  1.9 1.2 copy-start.1
  3.1 0.9 copy-start.2
  4.0 0.9 copy-start.3
  5.0 0.9 copy-start.4

commit v3 on v2

v3 whole, which is shorter than its diff:
```python
import functools

import jax
import jax.numpy as jnp
from jax import lax
from jax.experimental import pallas as pl
from jax.experimental.pallas import tpu as pltpu
from jax.sharding import PartitionSpec as P

MESH = pl.DeviceIdType.MESH

first_beta = 0.9
second_beta = 0.95
learn_rate = 0.01
decay_rate = 0.1
epsilon = 1e-08
first_fix = 1.0 - 0.9**20
second_fix = 1.0 - 0.95**20

PIECES = 2
WIDTH = 1024 // PIECES
PARTS = 2
SR = 64 // PARTS
SLICES = PIECES * PARTS
STEP, HOP = 1.4, 4.5
TIMES = (6.0, 14.0, 18.0, 24.0, 30.0, 1.0, 1.0)


def kernel(
    tok, cot, master, moment, second,
    master_new, moment_new, second_new, weights,
    tg, cg, part, core_in, z_in, grad, state, ssem, rsem, lsem,
):
    fetch = [
        pltpu.make_async_copy(ref, state.at[i], lsem.at[2 + i])
        for i, ref in enumerate((master, moment, second))
    ]
    for f in fetch:
        f.start()
    node, l = lax.axis_index("node"), lax.axis_index("local")
    c = node % 2
    y = (node // 2) % 4
    h = (node // 8) % 2
    x = node // 16
    z = h * 4 + l

    def dev(dx=0, dy=0, dz=0, dc=0):
        zz = (z + dz + 8) % 8
        xx, yy, cc = (x + dx + 4) % 4, (y + dy + 4) % 4, (c + dc) % 2
        return (((xx * 2 + zz // 4) * 4 + yy) * 2 + cc, zz % 4)

    count = [0]

    def ids(n=1):
        first = count[0]
        count[0] += n
        return first

    def rcopy(src, dst, sid, to):
        return pltpu.make_async_remote_copy(
            src_ref=src, dst_ref=dst, send_sem=ssem.at[sid], recv_sem=rsem.at[sid],
            device_id=to, device_id_type=MESH,
        )

    sent = []

    def start(cp):
        cp.start()
        sent.append(cp)

    barrier = pltpu.get_barrier_semaphore()
    peers = [dev(dx=d) for d in (1, 2, 3)] + [dev(dy=d) for d in (1, 2, 3)]
    peers += [dev(dz=1), dev(dz=-1), dev(dz=4), dev(dc=1)]
    for p in peers:
        pl.semaphore_signal(barrier, inc=1, device_id=p, device_id_type=MESH)
    pl.semaphore_wait(barrier, len(peers))

    def cols(b):
        return pl.ds(pl.multiple_of(b * 1024, 1024), 1024)

    def slot(buf, ry, rx, lo=0, n=128):
        return buf.at[ry, pl.ds(rx * 128 + lo, n)]

    own_t, own_c = tok.at[:, cols(x)], cot.at[:, cols(y)]
    lt = pltpu.make_async_copy(own_t, slot(tg, 0, 0), lsem.at[0])
    lc = pltpu.make_async_copy(own_c, slot(cg, 0, 0), lsem.at[1])
    lt.start()
    lc.start()
    ta, ca = {}, {}
    for d in (1, 3, 2):
        r = (4 - d) % 4
        ta[r] = rcopy(tok.at[:, cols((x + d) % 4)], slot(tg, 0, r), ids(), dev(dx=d))
        ca[r] = rcopy(cot.at[:, cols((y + d) % 4)], slot(cg, r, 0), ids(), dev(dy=d))
        start(ta[r])
        start(ca[r])
    tp, tm, cp_, cm = {}, {}, {}, {}

    def spread_t(rx):
        src = own_t if rx == 0 else slot(tg, 0, rx)
        tp[rx] = rcopy(src, slot(tg, 3, rx), ids(), dev(dy=1))
        tm[rx] = rcopy(src, slot(tg, 1, rx), ids(), dev(dy=-1))
        start(tp[rx])
        start(tm[rx])

    def spread_c(ry):
        src = own_c if ry == 0 else slot(cg, ry, 0)
        cp_[ry] = rcopy(src, slot(cg, ry, 3), ids(), dev(dx=1))
        cm[ry] = rcopy(src, slot(cg, ry, 1), ids(), dev(dx=-1))
        start(cp_[ry])
        start(cm[ry])

    spread_t(0)
    spread_c(0)
    for r in (3, 1, 2):
        ta[r].wait_recv()
        spread_t(r)
        ca[r].wait_recv()
        spread_c(r)
    tfp, tfm, cfp, cfm = {}, {}, {}, {}
    lt.wait()
    lc.wait()

    def forward(r):
        tp[r].wait_recv()
        tfp[r] = rcopy(slot(tg, 3, r, 0, 64), slot(tg, 2, r, 0, 64), ids(), dev(dy=1))
        start(tfp[r])
        cp_[r].wait_recv()
        cfp[r] = rcopy(slot(cg, r, 3, 0, 64), slot(cg, r, 2, 0, 64), ids(), dev(dx=1))
        start(cfp[r])
        tm[r].wait_recv()
        tfm[r] = rcopy(slot(tg, 1, r, 64, 64), slot(tg, 2, r, 64, 64), ids(), dev(dy=-1))
        start(tfm[r])
        cm[r].wait_recv()
        cfm[r] = rcopy(slot(cg, r, 1, 64, 64), slot(cg, r, 2, 64, 64), ids(), dev(dx=-1))
        start(cfm[r])

    def tile(ry, m, p, first):
        rows, out = pl.ds(pl.multiple_of(m * 256, 256), 256), pl.ds(p * WIDTH, WIDTH)
        got = lax.dot_general(
            tg[ry, :, rows], cg[ry, :, out], (((0,), (0,)), ((), ())),
            preferred_element_type=jnp.float32,
        )
        part[rows, out] = got if first else part[rows, out] + got

    def matmul(ry, first):
        @pl.loop(0, 4)
        def _(m):
            for p in range(PIECES):
                tile(ry, m, p, first)

    forward(0)
    forward(3)
    cfp[0].wait_recv()
    cfm[0].wait_recv()
    matmul(0, True)
    forward(1)
    cfp[3].wait_recv()
    cfm[3].wait_recv()
    forward(2)
    matmul(3, False)
    cfp[1].wait_recv()
    cfm[1].wait_recv()
    matmul(1, False)
    cfp[2].wait_recv()
    cfm[2].wait_recv()
    for r in range(4):
        tfp[r].wait_recv()
        tfm[r].wait_recv()

    core_id = ids(8 * PIECES)

    def block(hh, yy, cc, lo=0, n=64):
        return pl.ds(pl.multiple_of(hh * 512 + yy * 128 + cc * 64 + lo, n), n)

    def wide(p):
        return pl.ds(p * WIDTH, WIDTH)

    def core_copy(hh, yy, p):
        return rcopy(
            part.at[block(hh, yy, 1 - c), wide(p)], core_in.at[hh, yy, :, wide(p)],
            core_id + (p * 2 + hh) * 4 + yy, dev(dc=1),
        )

    events = []

    def at(when, what, place=None):
        events.append((when, len(events), place, what))

    r = (z - y + 8) % 8
    q = r % 4
    end = q == 0
    up = jnp.where(r < 4, 1, 0)
    z_id = [ids(4 * SLICES), ids(4 * SLICES)]
    g_id = ids(4 * SLICES)
    order = ((2, 3, 0, 1), (0, 1, 2, 3))

    for p in range(PIECES):
        for k in range(4):
            half = jnp.where(end, (up, up, 1 - up, 1 - up)[k], (up, 1 - up, up, 1 - up)[k])
            pair = jnp.where(end, (0, 1, 0, 1)[k], (1, 0, 0, 1)[k])
            tile(2, half * 2 + pair, p, False)
            for b in range(2):
                core_copy(half, pair * 2 + b, p).start()

    def chunk(hh, s, yy):
        return block(hh, yy, c, (s % PARTS) * SR, SR), wide(s // PARTS)

    def z_copy(way, hh, s, yy):
        return rcopy(
            part.at[chunk(hh, s, yy)], z_in.at[way, s, yy],
            z_id[way] + s * 4 + yy, dev(dz=1 - 2 * way),
        )

    def g_copy(s, yy):
        return pltpu.make_async_remote_copy(
            src_ref=part.at[chunk(h, s, yy)], dst_ref=grad.at[s],
            send_sem=ssem.at[g_id + s * 4 + yy], recv_sem=rsem.at[g_id + s],
            device_id=(((x * 2 + h) * 4 + yy) * 2 + c, l), device_id_type=MESH,
        )

    def core_sum(hh, yy, p):
        core_copy(hh, yy, p).wait_recv()
        part[block(hh, yy, c), wide(p)] += core_in[hh, yy, :, wide(p)]

    def link(place, way, k):
        hh = up if way == 0 else 1 - up
        s, i = k // 4, k % 4
        yy = order[way][i]
        if s % PARTS == 0:
            core_sum(hh, yy, s // PARTS)
        if i >= 2 or place != (1 if way == 0 else 3):
            z_copy(way, hh, s, yy).wait_recv()
            rows, width = chunk(hh, s, yy)
            part[rows, width] += z_in[way, s, yy]
        z_copy(way, hh, s, yy).start()

    for place in (1, 2, 3):
        for way in range(2):
            for k in range(4 * SLICES):
                behind = place - 1 if way == 0 else 3 - place
                at(k * STEP + HOP * behind, functools.partial(link, place, way, k), place)

    def far(s, i, way):
        yy = order[way][i + 2]
        if s % PARTS == 0:
            core_sum(up, yy, s // PARTS)
        z_copy(way, up, s, yy).start()

    def last(s, yy):
        if s % PARTS == 0:
            core_sum(h, yy, s // PARTS)
        z_copy(0, h, s, yy).wait_recv()
        z_copy(1, h, s, yy).wait_recv()
        rows, width = chunk(h, s, yy)
        total = part[rows, width] + (z_in[0, s, yy] + z_in[1, s, yy])
        part[rows, width] = total

        @pl.when(yy == y)
        def _():
            grad[s] = total

        @pl.when(yy != y)
        def _():
            g_copy(s, yy).start()

    for s in range(SLICES):
        for i in range(2):
            for way in range(2):
                at(0 if s < PARTS else s * 2 * STEP, functools.partial(far, s, i, way), 0)
        for yy in range(4):
            at((s * 4 + yy) * STEP + 3 * HOP + 1, functools.partial(last, s, yy), 0)

    def adam(s):
        if s == 0:
            for f in fetch:
                f.wait()

        @pl.when(jnp.logical_not(end))
        def _():
            g_copy(s, 0).wait_recv()

        rows, width = pl.ds((s % PARTS) * SR, SR), wide(s // PARTS)
        g = grad[s]
        old = state[0, rows, width]
        m_new = first_beta * state[1, rows, width] + (1.0 - first_beta) * g
        s_new = second_beta * state[2, rows, width] + (1.0 - second_beta) * g * g
        update = m_new / first_fix / (jnp.sqrt(s_new / second_fix) + epsilon) + decay_rate * old
        new = old - learn_rate * update
        master_new[rows, width] = new
        moment_new[rows, width] = m_new
        second_new[rows, width] = s_new
        weights[x, h, y, c, rows, width] = new.astype(jnp.bfloat16)

    def da(d):
        return dev(dx=d * (1 - c), dy=d * c)

    def db(d):
        return dev(dx=d * c, dy=d * (1 - c))

    both = slice(None)
    side = dev(dc=1)
    side_id = ids()

    def spread(p):
        def unit(hh, a=0, b=0):
            xx = (x + a * (1 - c) + b * c + 4) % 4
            yy = (y + a * c + b * (1 - c) + 4) % 4
            return weights.at[xx, hh, yy, c, :, wide(p)]

        def pass_on(ref, to):
            cp = rcopy(ref, ref, ids(), to)
            start(cp)
            return cp

        def to_side(hh, a=0, b=0):
            rcopy(unit(hh, a, b), unit(hh, a, b), side_id, side).start()

        w_a, w_b, f_b, w_z = {}, {}, {}, {}

        def a_send(k):
            hh = (h, 1 - h)[k]
            for d in (1, -1, 2):
                w_a[k, d] = pass_on(unit(hh), da(d))

        def b_send(a, k, hh):
            for d in (1, -1):
                w_b[a, k, d] = pass_on(unit(hh, a), db(d))

        def first():
            for s in range(p * PARTS, (p + 1) * PARTS):
                adam(s)
            w_z[0] = pass_on(unit(h), dev(dz=4))
            a_send(0)
            b_send(0, 0, h)
            to_side(h)

        def second():
            w_z[0].wait_recv()
            a_send(1)
            b_send(0, 1, 1 - h)
            to_side(1 - h)

        def third(a):
            for k in range(2):
                w_a[k, 2 if a == 2 else -a].wait_recv()
            b_send(a, 0, both)
            to_side(both, a)

        def onward(a, d):
            for k in range(2 if a == 0 else 1):
                w_b[a, k, d].wait_recv()
            hh = h if d == 1 else 1 - h
            f_b[a, d] = pass_on(unit(hh, a, -d), db(d))
            to_side(both, a, -d)

        def finish(a):
            f_b[a, 1].wait_recv()
            f_b[a, -1].wait_recv()
            to_side(both, a, 2)

        P_ = functools.partial
        T = TIMES
        out = [(T[0], first), (T[1], second)]
        for i, a in enumerate((-1, 1, 2)):
            out.append((T[2] + i * T[5], P_(third, a)))
        for i, a in enumerate((0, -1, 1, 2)):
            for d in (1, -1):
                out.append((T[3] + i * T[6], P_(onward, a, d)))
            out.append((T[4] + i * T[6], P_(finish, a)))
        return out

    for p in range(PIECES):
        ready = (p + 1) * 4 * PARTS * STEP + 3 * HOP + 1
        for when, stage in spread(p):
            at(ready + when, stage)

    events.sort(key=lambda e: e[:2])
    slots = sorted({int(e[0]) for e in events})
    for slot_ in slots:
        now = [e for e in events if int(e[0]) == slot_]
        for place in range(4):
            todo = [e[3] for e in now if e[2] == place]
            if todo:
                @pl.when(q == place)
                def _():
                    for what in todo:
                        what()
        for e in now:
            if e[2] is None:
                e[3]()

    all_side = rcopy(weights.at[:, :, :, c], weights.at[:, :, :, 1 - c], side_id, side)
    all_side.wait_recv()
    all_side.wait_send()
    assert count[0] == N_SEM, count[0]
    for cp in sent:
        cp.wait_send()
    for p in range(PIECES):
        for b in range(8):
            core_copy(b // 4, b % 4, p).wait_send()

    @pl.when(jnp.logical_not(end))
    def _():
        for s in range(SLICES):
            for yy in range(4):
                for way in range(2):
                    z_copy(way, 0, s, yy).wait_send()

    @pl.when(end)
    def _():
        for s in range(SLICES):
            for i in range(2):
                for way in range(2):
                    z_copy(way, up, s, order[way][i + 2]).wait_send()
            for yy in range(4):
                @pl.when(yy != y)
                def _():
                    g_copy(s, yy).wait_send()


def copy_kernel(*refs):
    sem = refs[-1]
    copies = [pltpu.make_async_copy(refs[i], refs[4 + i], sem.at[i]) for i in (3, 0, 1, 2)]
    for cp in copies:
        cp.start()
    for cp in copies:
        cp.wait()


def write_out(*arrays):
    return pl.pallas_call(
        copy_kernel,
        out_shape=[jax.ShapeDtypeStruct(a.shape, a.dtype) for a in arrays],
        in_specs=[pl.BlockSpec(memory_space=pltpu.VMEM)] * 4,
        out_specs=[pl.BlockSpec(memory_space=pltpu.HBM)] * 4,
        scratch_shapes=[pltpu.SemaphoreType.DMA((4,))],
        compiler_params=pltpu.CompilerParams(vmem_limit_bytes=2**20),
    )(*arrays)


N_SEM = 153
VMEM_GRANT = 36 * 2**20


def on_device(tokens, cotangent, master, moment, second):
    vmem, hbm = pl.BlockSpec(memory_space=pltpu.VMEM), pl.BlockSpec(memory_space=pl.ANY)
    f32 = jax.ShapeDtypeStruct((64, 1024), jnp.float32)
    out = pl.pallas_call(
        kernel,
        out_shape=(f32, f32, f32, jax.ShapeDtypeStruct((4, 2, 4, 2, 64, 1024), jnp.bfloat16)),
        in_specs=[hbm] * 5,
        out_specs=(vmem, vmem, vmem, vmem),
        scratch_shapes=[
            pltpu.VMEM((4, 512, 1024), jnp.bfloat16),
            pltpu.VMEM((4, 512, 1024), jnp.bfloat16),
            pltpu.VMEM((1024, 1024), jnp.float32),
            pltpu.VMEM((2, 4, 64, 1024), jnp.float32),
            pltpu.VMEM((2, SLICES, 4, SR, WIDTH), jnp.float32),
            pltpu.VMEM((SLICES, SR, WIDTH), jnp.float32),
            pltpu.VMEM((3, 64, 1024), jnp.float32),
            pltpu.SemaphoreType.DMA((N_SEM,)),
            pltpu.SemaphoreType.DMA((N_SEM,)),
            pltpu.SemaphoreType.DMA((5,)),
        ],
        compiler_params=pltpu.CompilerParams(
            collective_id=0, has_side_effects=True, vmem_limit_bytes=VMEM_GRANT
        ),
    )(tokens, cotangent, master, moment, second)
    return write_out(*out[:3], out[3].reshape(4096, 1024))


def solution(mesh):
    placed = (
        P(("node", "local"), None),
        P(("node", "local"), None),
        P("node", "local"),
        P("node", "local"),
        P("node", "local"),
    )
    return jax.shard_map(
        on_device,
        mesh=mesh,
        in_specs=placed,
        out_specs=(P("node", "local"), P("node", "local"), P("node", "local"), P(None, "local")),
        check_vma=False,
    )
```

time: 153 us -> 137 us (0.90)
  local copies, waits for them, and re-layouts: 15.2 us -> 5.29 us
  Pallas kernels: 137 us -> 130 us
    pallas_call x1, Pallas kernels: 137 us -> 127 us  [on_device(): pl.pallas_call(kernel, out_shape=(f32, f32, f32, jax.ShapeDtypeStruct((4,...]
    unnamed x14 -> x10, local copies, waits for them, and re-layouts: 15.2 us -> 5.29 us
    pallas_call x0 -> x1, Pallas kernels: none -> 3.66 us  [write_out(): pl.pallas_call(copy_kernel, out_shape=[jax.ShapeDtypeStruct(a.shape, a.dt...]
where the time goes in v3:
time: 137 us; the launch traced here: 136 us
  Pallas kernels  130 us (95%)
  local copies, waits for them, and re-layouts  5.29 us (4%)
    pallas_call x1, Pallas kernels, on_device(): pl.pallas_call(kernel, out_shape=(f32, f32, f32, jax.ShapeDtypeStruct((4,...  127 us
    unnamed x10, local copies, waits for them, and re-layouts  5.29 us
    pallas_call x1, Pallas kernels, write_out(): pl.pallas_call(copy_kernel, out_shape=[jax.ShapeDtypeStruct(a.shape, a.dt...  3.66 us

profile of v3, /device:TPU:1, one launch (start us, length us, event | category | flops | bytes accessed | tf_op | source)
XLA Modules:
  0.0 136.3 jit_solution(361476848274807227)
XLA Ops:
  0.6 0.0 copy-start
  0.6 1.2 copy-done
  1.9 0.0 copy-start.1
  1.9 1.2 copy-done.1
  3.1 0.0 copy-start.2
  3.1 0.9 copy-done.2
  4.0 0.0 copy-start.3
  4.0 0.9 copy-done.3
  5.0 0.0 copy-start.4
  5.0 0.9 copy-done.4
  5.9 126.7 %shard_map.84 = (f32[64,1024]{1,0:T(8,128)S(1)}, f32[64,1024]{1,0:T(8,128)S(1)}, f32[64,1024]{1,0:T(8,128)S(1)}, bf16[4,2,4,2,64,1024]{5,4,3,2,1,0:T(8,128)(2,1)S(1)}) custom-call(bf16[128,4096]{1,0:T(8,128)(2,1)S(1)} %copy-done, bf16[128,4096]{1,0:T(8,128)(2,1)S(1)} %copy-done.1, f32[64,1024]{1,0:T(8,128)S(1)} %copy-done.2, f32[64,1024]{1,0:T(8,128)S(1)} %copy-done.3, ...), custom_call_target="tpu_custom_call" | custom-call | tf_op jit(solution)/shard_map/pallas_call | solution.py:448
  132.7 3.7 %shard_map.85 = (f32[64,1024]{1,0:T(8,128)}, f32[64,1024]{1,0:T(8,128)}, f32[64,1024]{1,0:T(8,128)}, bf16[4096,1024]{1,0:T(8,128)(2,1)}) custom-call(f32[64,1024]{1,0:T(8,128)S(1)} %get-tuple-element.8.refs_0_, f32[64,1024]{1,0:T(8,128)S(1)} %get-tuple-element.9.refs_1_, f32[64,1024]{1,0:T(8,128)S(1)} %get-tuple-element.10.refs_2_, ...), custom_call_target="tpu_custom_call" | custom-call | tf_op jit(solution)/shard_map/pallas_call | solution.py:431
Async XLA Ops:
  0.6 1.2 copy-start
  1.9 1.2 copy-start.1
  3.1 0.9 copy-start.2
  4.0 0.9 copy-start.3
  5.0 0.9 copy-start.4

commit v4 on v3

v4 whole, which is shorter than its diff:
```python
import functools

import jax
import jax.numpy as jnp
from jax import lax
from jax.experimental import pallas as pl
from jax.experimental.pallas import tpu as pltpu
from jax.sharding import PartitionSpec as P

MESH = pl.DeviceIdType.MESH

first_beta = 0.9
second_beta = 0.95
learn_rate = 0.01
decay_rate = 0.1
epsilon = 1e-08
first_fix = 1.0 - 0.9**20
second_fix = 1.0 - 0.95**20

PIECES = 2
WIDTH = 1024 // PIECES
PARTS = 2
SR = 64 // PARTS
SLICES = PIECES * PARTS
QUADS = ((0, 0), (1, 0), (0, 1), (1, 1))
GATHER = (
    (0, 4, 5, 7, 9, 13, 16, 19, 20, 22, 23, 26),
    (14, 24, 25, 27, 31, 35, 38, 41, 42, 44, 45, 49),
)
CHAIN = (33, 52, 57.6, 63.2)
STEP, HOP = 1.4, 4.5
TIMES = (6.0, 14.0, 11.0, 20.0, 16.0, 25.0, 31.0, 1.0)


def kernel(
    tok, cot, master, moment, second,
    master_new, moment_new, second_new, weights,
    tg, cg, part, core_in, z_in, grad, state, ssem, rsem, lsem,
):
    fetch = [
        pltpu.make_async_copy(ref, state.at[i], lsem.at[6 + i])
        for i, ref in enumerate((master, moment, second))
    ]
    for f in fetch:
        f.start()
    node, l = lax.axis_index("node"), lax.axis_index("local")
    c = lax.rem(node, 2)
    y = lax.rem(lax.div(node, 2), 4)
    h = lax.rem(lax.div(node, 8), 2)
    x = lax.div(node, 16)
    z = h * 4 + l

    def around(v, n):
        return [v] + [lax.rem(v + d, n) for d in range(1, n)]

    xs, ys, zs = around(x, 4), around(y, 4), around(z, 8)

    def node_of(xx, hh, yy, cc):
        return ((xx * 2 + hh) * 4 + yy) * 2 + cc

    peer = {("x", d): (node_of(xs[d], h, y, c), l) for d in (1, 2, 3)}
    peer |= {("y", d): (node_of(x, h, ys[d], c), l) for d in (1, 2, 3)}
    peer |= {("z", d): (node_of(x, lax.div(zs[d], 4), y, c), lax.rem(zs[d], 4)) for d in (1, 7, 4)}
    peer["core", 1] = (node_of(x, h, y, 1 - c), l)
    for d in (1, 2, 3):
        for axis, one, two in (("a", "x", "y"), ("b", "y", "x")):
            peer[axis, d] = (jnp.where(c == 0, peer[one, d][0], peer[two, d][0]), l)
    row_peer = [(node_of(x, h, yy, c), l) for yy in range(4)]
    place_of = {
        (a, b): (jnp.where(c == 0, xs[a % 4], xs[b % 4]), jnp.where(c == 0, ys[b % 4], ys[a % 4]))
        for a in (0, -1, 1, 2) for b in (0, -1, 1, 2)
    }

    def dev(dx=0, dy=0, dz=0, dc=0):
        if dx:
            return peer["x", dx % 4]
        if dy:
            return peer["y", dy % 4]
        return peer["z", dz % 8] if dz else peer["core", dc]

    count = [0]

    def ids(n=1):
        first = count[0]
        count[0] += n
        return first

    CORE, CHAIN_Z, ROW, WEIGHTS, SIDE = range(2, 7)

    def rcopy(kind, src, dst, sid, to):
        return pltpu.make_async_remote_copy(
            src_ref=src, dst_ref=dst, send_sem=ssem.at[kind], recv_sem=rsem.at[sid],
            device_id=to, device_id_type=MESH,
        )

    def all_sent(kind, kib):
        rows = part.at[pl.ds(0, kib // 4)]
        rcopy(kind, rows, rows, 0, dev(dc=1)).wait_send()

    barrier = pltpu.get_barrier_semaphore()
    peers = [dev(dx=d) for d in (1, 2, 3)] + [dev(dy=d) for d in (1, 2, 3)]
    peers += [dev(dz=1), dev(dz=-1), dev(dz=4), dev(dc=1)]
    for p in peers:
        pl.semaphore_signal(barrier, inc=1, device_id=p, device_id_type=MESH)
    pl.semaphore_wait(barrier, len(peers))

    events = []

    def at(when, what, place=None):
        events.append((when, len(events), place, what))

    def slot(buf, u, ry, rx, lo=0, n=128):
        return buf.at[u, ry, pl.ds(rx * 128 + lo, n)]

    def t_cols(b, hh, u):
        return tok.at[:, pl.ds(pl.multiple_of(b * 1024 + hh * 512 + u * 256, 256), 256)]

    def c_cols(b, u):
        return cot.at[:, pl.ds(pl.multiple_of(b * 1024 + u * 512, 512), 512)]

    ta, ca, tp, tm, cp_, cm, tfp, tfm, cfp, cfm = ({} for _ in range(10))

    def spread_t(u, r):
        src = slot(tg, u, 0, r)
        tp[u, r] = rcopy(u, src, slot(tg, u, 3, r), ids(), dev(dy=1))
        tm[u, r] = rcopy(u, src, slot(tg, u, 1, r), ids(), dev(dy=-1))
        tp[u, r].start()
        tm[u, r].start()

    def spread_c(u, r):
        src = c_cols(y, u) if r == 0 else slot(cg, u, r, 0)
        cp_[u, r] = rcopy(u, src, slot(cg, u, r, 3), ids(), dev(dx=1))
        cm[u, r] = rcopy(u, src, slot(cg, u, r, 1), ids(), dev(dx=-1))
        cp_[u, r].start()
        cm[u, r].start()

    def gather_first(u):
        own = [
            pltpu.make_async_copy(
                t_cols(x, hh, u), tg.at[u, 0, pl.ds(0, 128), pl.ds(hh * 256, 256)], lsem.at[3 * u + hh]
            )
            for hh in range(2)
        ]
        own.append(pltpu.make_async_copy(c_cols(y, u), slot(cg, u, 0, 0), lsem.at[3 * u + 2]))
        for cp in own:
            cp.start()
        for d in (1, 3, 2):
            r = (4 - d) % 4
            ta[u, r] = rcopy(u, slot(tg, u, 0, r), slot(tg, u, 0, r), ids(), dev(dx=d))
            for hh in range(2):
                rcopy(u,
                    t_cols(xs[d], hh, u), tg.at[u, 0, pl.ds(r * 128, 128), pl.ds(hh * 256, 256)],
                    count[0] - 1, dev(dx=d),
                ).start()
            ca[u, r] = rcopy(u, c_cols(ys[d], u), slot(cg, u, r, 0), ids(), dev(dy=d))
            ca[u, r].start()
        spread_c(u, 0)
        for cp in own:
            cp.wait()
        spread_t(u, 0)

    def gather_next(u, r):
        ta[u, r].wait_recv()
        spread_t(u, r)
        ca[u, r].wait_recv()
        spread_c(u, r)

    def forward(u, r):
        tp[u, r].wait_recv()
        tfp[u, r] = rcopy(u, slot(tg, u, 3, r, 0, 64), slot(tg, u, 2, r, 0, 64), ids(), dev(dy=1))
        tfp[u, r].start()
        cp_[u, r].wait_recv()
        cfp[u, r] = rcopy(u, slot(cg, u, r, 3, 0, 64), slot(cg, u, r, 2, 0, 64), ids(), dev(dx=1))
        cfp[u, r].start()
        tm[u, r].wait_recv()
        tfm[u, r] = rcopy(u, slot(tg, u, 1, r, 64, 64), slot(tg, u, 2, r, 64, 64), ids(), dev(dy=-1))
        tfm[u, r].start()
        cm[u, r].wait_recv()
        cfm[u, r] = rcopy(u, slot(cg, u, r, 1, 64, 64), slot(cg, u, r, 2, 64, 64), ids(), dev(dx=-1))
        cfm[u, r].start()

    def tile(u, p, ry, hh):
        rows = pl.ds(pl.multiple_of(hh * 512 + u * 256, 256), 256)
        cols = pl.ds(pl.multiple_of(hh * 256, 256), 256)
        got = lax.dot_general(
            tg[u, ry, :, cols], cg[p, ry], (((0,), (0,)), ((), ())),
            preferred_element_type=jnp.float32,
        )
        part[rows, wide(p)] = got if ry == 0 else part[rows, wide(p)] + got

    def product(half, ry):
        cfp[half, ry].wait_recv()
        cfm[half, ry].wait_recv()
        for u, p in QUADS[:1] if half == 0 else QUADS[1:]:
            @pl.loop(0, 2)
            def _(hh):
                tile(u, p, ry, hh)

    def product_last(half):
        cfp[half, 2].wait_recv()
        cfm[half, 2].wait_recv()
        for r in range(4):
            tfp[half, r].wait_recv()
            tfm[half, r].wait_recv()
        for u, p in QUADS[:1] if half == 0 else QUADS[1:]:
            for hh in (up, 1 - up):
                tile(u, p, 2, hh)
                for yy in (2 * u, 2 * u + 1):
                    core_copy(hh, yy, p).start()

    for u in range(2):
        G = GATHER[u]
        at(G[0], functools.partial(gather_first, u))
        for i, r in enumerate((3, 1, 2)):
            at(G[1 + i], functools.partial(gather_next, u, r))
        for i, r in enumerate((0, 3, 1, 2)):
            at(G[4 + i], functools.partial(forward, u, r))
        for i, r in enumerate((0, 3, 1)):
            at(G[8 + i], functools.partial(product, u, r))
        at(G[11], functools.partial(product_last, u))

    core_id = ids(8 * PIECES)

    def block(hh, yy, cc, lo=0, n=64):
        return pl.ds(pl.multiple_of(hh * 512 + yy * 128 + cc * 64 + lo, n), n)

    def wide(p):
        return pl.ds(p * WIDTH, WIDTH)

    def core_copy(hh, yy, p):
        return rcopy(
            CORE, part.at[block(hh, yy, 1 - c), wide(p)], core_in.at[hh, yy, :, wide(p)],
            core_id + (p * 2 + hh) * 4 + yy, dev(dc=1),
        )

    r = lax.rem(z - y + 8, 8)
    q = lax.rem(r, 4)
    end = q == 0
    up = jnp.where(r < 4, 1, 0)
    z_id = [ids(4 * SLICES), ids(4 * SLICES)]
    g_id = ids(SLICES)

    def chunk(hh, s, yy):
        return block(hh, yy, c, (s % PARTS) * SR, SR), wide(s // PARTS)

    def z_copy(way, hh, s, yy):
        return rcopy(
            CHAIN_Z, part.at[chunk(hh, s, yy)], z_in.at[way, s, yy],
            z_id[way] + s * 4 + yy, dev(dz=1 - 2 * way),
        )

    def g_copy(s, yy):
        return pltpu.make_async_remote_copy(
            src_ref=part.at[chunk(h, s, yy)], dst_ref=grad.at[s],
            send_sem=ssem.at[ROW], recv_sem=rsem.at[g_id + s],
            device_id=row_peer[yy], device_id_type=MESH,
        )

    def core_sum(hh, yy, p):
        core_copy(hh, yy, p).wait_recv()
        part[block(hh, yy, c), wide(p)] += core_in[hh, yy, :, wide(p)]

    def parts_of(j, way):
        u, p = QUADS[j]
        return [(p * PARTS + s, 2 * u + (i + 1 - way) % 2) for s in range(PARTS) for i in range(2)]

    def link(place, way, j, i):
        hh = up if way == 0 else 1 - up
        s, yy = parts_of(j, way)[i]
        if s % PARTS == 0:
            core_sum(hh, yy, s // PARTS)
        if i % 2 or place != (1 if way == 0 else 3):
            z_copy(way, hh, s, yy).wait_recv()
            rows, width = chunk(hh, s, yy)
            part[rows, width] += z_in[way, s, yy]
        z_copy(way, hh, s, yy).start()

    def far(j, i, way):
        s, yy = parts_of(j, way)[i]
        if s % PARTS == 0:
            core_sum(up, yy, s // PARTS)
        z_copy(way, up, s, yy).start()

    def last(s, yy):
        if s % PARTS == 0:
            core_sum(h, yy, s // PARTS)
        z_copy(0, h, s, yy).wait_recv()
        z_copy(1, h, s, yy).wait_recv()
        rows, width = chunk(h, s, yy)
        total = part[rows, width] + (z_in[0, s, yy] + z_in[1, s, yy])
        part[rows, width] = total

        @pl.when(yy == y)
        def _():
            grad[s] = total

        @pl.when(yy != y)
        def _():
            g_copy(s, yy).start()

    for j in range(4):
        for i in range(2 * PARTS):
            for way in range(2):
                for place in (1, 2, 3):
                    behind = place - 1 if way == 0 else 3 - place
                    at(CHAIN[j] + i * STEP + HOP * behind, functools.partial(link, place, way, j, i), place)
                if i % 2:
                    at(CHAIN[j] + i * STEP - STEP, functools.partial(far, j, i, way), 0)
            at(CHAIN[j] + i * STEP + 3 * HOP + 1, functools.partial(last, *parts_of(j, 1)[i]), 0)

    def adam(s):
        if s == 0:
            for f in fetch:
                f.wait()

        @pl.when(jnp.logical_not(end))
        def _():
            g_copy(s, 0).wait_recv()

        rows, width = pl.ds((s % PARTS) * SR, SR), wide(s // PARTS)
        g = grad[s]
        old = state[0, rows, width]
        m_new = first_beta * state[1, rows, width] + (1.0 - first_beta) * g
        s_new = second_beta * state[2, rows, width] + (1.0 - second_beta) * g * g
        update = m_new / first_fix / (jnp.sqrt(s_new / second_fix) + epsilon) + decay_rate * old
        new = old - learn_rate * update
        master_new[rows, width] = new
        moment_new[rows, width] = m_new
        second_new[rows, width] = s_new
        weights[x, h, y, c, rows, width] = new.astype(jnp.bfloat16)

    def da(d):
        return peer["a", d % 4]

    def db(d):
        return peer["b", d % 4]

    both = slice(None)
    side = dev(dc=1)
    side_id = ids()

    def spread(p):
        def unit(hh, a=0, b=0):
            xx, yy = place_of[a, b]
            return weights.at[xx, hh, yy, c, :, wide(p)]

        def pass_on(ref, to):
            cp = rcopy(WEIGHTS, ref, ref, ids(), to)
            cp.start()
            return cp

        def to_side(hh, a=0, b=0):
            rcopy(SIDE, unit(hh, a, b), unit(hh, a, b), side_id, side).start()

        w_a, w_b, f_b, w_z = {}, {}, {}, {}

        def a_send(k):
            hh = (h, 1 - h)[k]
            for d in (1, -1, 2):
                w_a[k, d] = pass_on(unit(hh), da(d))

        def b_send(a, k, hh):
            for d in (1, -1):
                w_b[a, k, d] = pass_on(unit(hh, a), db(d))

        def first():
            for s in range(p * PARTS, (p + 1) * PARTS):
                adam(s)
            w_z[0] = pass_on(unit(h), dev(dz=4))
            a_send(0)
            b_send(0, 0, h)
            to_side(h)

        def second():
            w_z[0].wait_recv()
            a_send(1)
            b_send(0, 1, 1 - h)
            to_side(1 - h)

        def third(a, k):
            w_a[k, 2 if a == 2 else -a].wait_recv()
            b_send(a, k, (h, 1 - h)[k])
            if k == 1:
                to_side(both, a)

        def onward(a, k):
            d = (1, -1)[k]
            w_b[a, k, d].wait_recv()
            ref = unit((h, 1 - h)[k], a, -d)
            f_b[a, d] = pass_on(ref, db(d))
            if k == 1:
                w_b[a, 0, -1].wait_recv()
                to_side(both, a, 1)
                w_b[a, 1, 1].wait_recv()
                to_side(both, a, -1)

        def finish(a):
            f_b[a, 1].wait_recv()
            f_b[a, -1].wait_recv()
            to_side(both, a, 2)

        P_ = functools.partial
        T = TIMES
        out = [(T[0], first), (T[1], second)]
        for k in range(2):
            for i, a in enumerate((-1, 1, 2)):
                out.append((T[2 + k] + i * T[7], P_(third, a, k)))
            for i, a in enumerate((0, -1, 1, 2)):
                out.append((T[4 + k] + i * T[7], P_(onward, a, k)))
        for i, a in enumerate((0, -1, 1, 2)):
            out.append((T[6] + i * T[7], P_(finish, a)))
        return out

    for p in range(PIECES):
        ready = CHAIN[2 * p + 1] + 2 * PARTS * STEP + 3 * HOP + 1
        for when, stage in spread(p):
            at(ready + when, stage)

    events.sort(key=lambda e: e[:2])
    slots = sorted({int(e[0]) for e in events})
    for slot_ in slots:
        now = [e for e in events if int(e[0]) == slot_]
        for place in range(4):
            todo = [e[3] for e in now if e[2] == place]
            if todo:
                @pl.when(q == place)
                def _():
                    for what in todo:
                        what()
        for e in now:
            if e[2] is None:
                e[3]()

    all_side = rcopy(SIDE, weights.at[:, :, :, c], weights.at[:, :, :, 1 - c], side_id, side)
    all_side.wait_recv()
    all_side.wait_send()
    assert count[0] == N_SEM, count[0]
    for u in range(2):
        all_sent(u, 6 * 128 + 16 * 128 + 16 * 64)
    all_sent(CORE, 16 * 128)
    all_sent(WEIGHTS, 62 * 64)

    @pl.when(jnp.logical_not(end))
    def _():
        all_sent(CHAIN_Z, 32 * 64)

    @pl.when(end)
    def _():
        all_sent(CHAIN_Z, 16 * 64)
        all_sent(ROW, 12 * 64)


def copy_kernel(*refs):
    sem = refs[-1]
    copies = [pltpu.make_async_copy(refs[i], refs[4 + i], sem.at[i]) for i in (3, 0, 1, 2)]
    for cp in copies:
        cp.start()
    for cp in copies:
        cp.wait()


def write_out(*arrays):
    return pl.pallas_call(
        copy_kernel,
        out_shape=[jax.ShapeDtypeStruct(a.shape, a.dtype) for a in arrays],
        in_specs=[pl.BlockSpec(memory_space=pltpu.VMEM)] * 4,
        out_specs=[pl.BlockSpec(memory_space=pltpu.HBM)] * 4,
        scratch_shapes=[pltpu.SemaphoreType.DMA((4,))],
        compiler_params=pltpu.CompilerParams(vmem_limit_bytes=2**20),
    )(*arrays)


N_SEM = 191
VMEM_GRANT = 36 * 2**20


def on_device(tokens, cotangent, master, moment, second):
    vmem, hbm = pl.BlockSpec(memory_space=pltpu.VMEM), pl.BlockSpec(memory_space=pl.ANY)
    f32 = jax.ShapeDtypeStruct((64, 1024), jnp.float32)
    out = pl.pallas_call(
        kernel,
        out_shape=(f32, f32, f32, jax.ShapeDtypeStruct((4, 2, 4, 2, 64, 1024), jnp.bfloat16)),
        in_specs=[hbm] * 5,
        out_specs=(vmem, vmem, vmem, vmem),
        scratch_shapes=[
            pltpu.VMEM((2, 4, 512, 512), jnp.bfloat16),
            pltpu.VMEM((2, 4, 512, 512), jnp.bfloat16),
            pltpu.VMEM((1024, 1024), jnp.float32),
            pltpu.VMEM((2, 4, 64, 1024), jnp.float32),
            pltpu.VMEM((2, SLICES, 4, SR, WIDTH), jnp.float32),
            pltpu.VMEM((SLICES, SR, WIDTH), jnp.float32),
            pltpu.VMEM((3, 64, 1024), jnp.float32),
            pltpu.SemaphoreType.DMA((7,)),
            pltpu.SemaphoreType.DMA((N_SEM,)),
            pltpu.SemaphoreType.DMA((9,)),
        ],
        compiler_params=pltpu.CompilerParams(
            collective_id=0, has_side_effects=True, vmem_limit_bytes=VMEM_GRANT
        ),
    )(tokens, cotangent, master, moment, second)
    return write_out(*out[:3], out[3].reshape(4096, 1024))


def solution(mesh):
    placed = (
        P(("node", "local"), None),
        P(("node", "local"), None),
        P("node", "local"),
        P("node", "local"),
        P("node", "local"),
    )
    return jax.shard_map(
        on_device,
        mesh=mesh,
        in_specs=placed,
        out_specs=(P("node", "local"), P("node", "local"), P("node", "local"), P(None, "local")),
        check_vma=False,
    )
```

time: 137 us -> 133 us (0.971)
  Pallas kernels: 130 us -> 127 us
    pallas_call x1, Pallas kernels: 127 us -> 123 us  [on_device(): pl.pallas_call(kernel, out_shape=(f32, f32, f32, jax.ShapeDtypeStruct((4,...]
where the time goes in v4:
time: 133 us
  Pallas kernels  127 us (95%)
  local copies, waits for them, and re-layouts  5.29 us (4%)
    pallas_call x1, Pallas kernels, on_device(): pl.pallas_call(kernel, out_shape=(f32, f32, f32, jax.ShapeDtypeStruct((4,...  123 us
    unnamed x10, local copies, waits for them, and re-layouts  5.29 us
    pallas_call x1, Pallas kernels, write_out(): pl.pallas_call(copy_kernel, out_shape=[jax.ShapeDtypeStruct(a.shape, a.dt...  3.66 us

profile of v4, /device:TPU:1, one launch (start us, length us, event | category | flops | bytes accessed | tf_op | source)
XLA Modules:
  0.0 132.9 jit_solution(11032136087660356223)
XLA Ops:
  0.6 0.0 copy-start
  0.6 1.2 copy-done
  1.9 0.0 copy-start.1
  1.9 1.2 copy-done.1
  3.1 0.0 copy-start.2
  3.1 0.9 copy-done.2
  4.0 0.0 copy-start.3
  4.0 0.9 copy-done.3
  5.0 0.0 copy-start.4
  5.0 0.9 copy-done.4
  5.9 123.3 %shard_map.84 = (f32[64,1024]{1,0:T(8,128)S(1)}, f32[64,1024]{1,0:T(8,128)S(1)}, f32[64,1024]{1,0:T(8,128)S(1)}, bf16[4,2,4,2,64,1024]{5,4,3,2,1,0:T(8,128)(2,1)S(1)}) custom-call(bf16[128,4096]{1,0:T(8,128)(2,1)S(1)} %copy-done, bf16[128,4096]{1,0:T(8,128)(2,1)S(1)} %copy-done.1, f32[64,1024]{1,0:T(8,128)S(1)} %copy-done.2, f32[64,1024]{1,0:T(8,128)S(1)} %copy-done.3, ...), custom_call_target="tpu_custom_call" | custom-call | tf_op jit(solution)/shard_map/pallas_call | solution.py:480
  129.2 3.7 %shard_map.85 = (f32[64,1024]{1,0:T(8,128)}, f32[64,1024]{1,0:T(8,128)}, f32[64,1024]{1,0:T(8,128)}, bf16[4096,1024]{1,0:T(8,128)(2,1)}) custom-call(f32[64,1024]{1,0:T(8,128)S(1)} %get-tuple-element.8.refs_0_, f32[64,1024]{1,0:T(8,128)S(1)} %get-tuple-element.9.refs_1_, f32[64,1024]{1,0:T(8,128)S(1)} %get-tuple-element.10.refs_2_, ...), custom_call_target="tpu_custom_call" | custom-call | tf_op jit(solution)/shard_map/pallas_call | solution.py:463
Async XLA Ops:
  0.6 1.2 copy-start
  1.9 1.2 copy-start.1
  3.1 0.9 copy-start.2
  4.0 0.9 copy-start.3
  5.0 0.9 copy-start.4

commit v5 on v4

--- a/solution.py
+++ b/solution.py
@@ -19,7 +19,7 @@
 
 PIECES = 2
 WIDTH = 1024 // PIECES
-PARTS = 2
+PARTS = 4
 SR = 64 // PARTS
 SLICES = PIECES * PARTS
 QUADS = ((0, 0), (1, 0), (0, 1), (1, 1))
@@ -28,7 +28,7 @@
     (14, 24, 25, 27, 31, 35, 38, 41, 42, 44, 45, 49),
 )
 CHAIN = (33, 52, 57.6, 63.2)
-STEP, HOP = 1.4, 4.5
+STEP, HOP = 0.7, 5.2
 TIMES = (6.0, 14.0, 11.0, 20.0, 16.0, 25.0, 31.0, 1.0)
 
 
@@ -118,7 +118,7 @@
     def c_cols(b, u):
         return cot.at[:, pl.ds(pl.multiple_of(b * 1024 + u * 512, 512), 512)]
 
-    ta, ca, tp, tm, cp_, cm, tfp, tfm, cfp, cfm = ({} for _ in range(10))
+    ta, ca, tp, tm, cp_, cm, tf, cf = ({} for _ in range(8))
 
     def spread_t(u, r):
         src = slot(tg, u, 0, r)
@@ -166,18 +166,17 @@
         spread_c(u, r)
 
     def forward(u, r):
+        tf[u, r] = rcopy(u, slot(tg, u, 2, r), slot(tg, u, 2, r), ids(), dev(dy=1))
+        cf[u, r] = rcopy(u, slot(cg, u, r, 2), slot(cg, u, r, 2), ids(), dev(dx=1))
+        t_id, c_id = count[0] - 2, count[0] - 1
         tp[u, r].wait_recv()
-        tfp[u, r] = rcopy(u, slot(tg, u, 3, r, 0, 64), slot(tg, u, 2, r, 0, 64), ids(), dev(dy=1))
-        tfp[u, r].start()
+        rcopy(u, slot(tg, u, 3, r, 0, 64), slot(tg, u, 2, r, 0, 64), t_id, dev(dy=1)).start()
         cp_[u, r].wait_recv()
-        cfp[u, r] = rcopy(u, slot(cg, u, r, 3, 0, 64), slot(cg, u, r, 2, 0, 64), ids(), dev(dx=1))
-        cfp[u, r].start()
+        rcopy(u, slot(cg, u, r, 3, 0, 64), slot(cg, u, r, 2, 0, 64), c_id, dev(dx=1)).start()
         tm[u, r].wait_recv()
-        tfm[u, r] = rcopy(u, slot(tg, u, 1, r, 64, 64), slot(tg, u, 2, r, 64, 64), ids(), dev(dy=-1))
-        tfm[u, r].start()
+        rcopy(u, slot(tg, u, 1, r, 64, 64), slot(tg, u, 2, r, 64, 64), t_id, dev(dy=-1)).start()
         cm[u, r].wait_recv()
-        cfm[u, r] = rcopy(u, slot(cg, u, r, 1, 64, 64), slot(cg, u, r, 2, 64, 64), ids(), dev(dx=-1))
-        cfm[u, r].start()
+        rcopy(u, slot(cg, u, r, 1, 64, 64), slot(cg, u, r, 2, 64, 64), c_id, dev(dx=-1)).start()
 
     def tile(u, p, ry, hh):
         rows = pl.ds(pl.multiple_of(hh * 512 + u * 256, 256), 256)
@@ -189,19 +188,16 @@
         part[rows, wide(p)] = got if ry == 0 else part[rows, wide(p)] + got
 
     def product(half, ry):
-        cfp[half, ry].wait_recv()
-        cfm[half, ry].wait_recv()
+        cf[half, ry].wait_recv()
         for u, p in QUADS[:1] if half == 0 else QUADS[1:]:
             @pl.loop(0, 2)
             def _(hh):
                 tile(u, p, ry, hh)
 
     def product_last(half):
-        cfp[half, 2].wait_recv()
-        cfm[half, 2].wait_recv()
+        cf[half, 2].wait_recv()
         for r in range(4):
-            tfp[half, r].wait_recv()
-            tfm[half, r].wait_recv()
+            tf[half, r].wait_recv()
         for u, p in QUADS[:1] if half == 0 else QUADS[1:]:
             for hh in (up, 1 - up):
                 tile(u, p, 2, hh)
@@ -344,15 +340,15 @@
             xx, yy = place_of[a, b]
             return weights.at[xx, hh, yy, c, :, wide(p)]
 
-        def pass_on(ref, to):
-            cp = rcopy(WEIGHTS, ref, ref, ids(), to)
+        def pass_on(ref, to, sid=None):
+            cp = rcopy(WEIGHTS, ref, ref, ids() if sid is None else sid, to)
             cp.start()
             return cp
 
         def to_side(hh, a=0, b=0):
             rcopy(SIDE, unit(hh, a, b), unit(hh, a, b), side_id, side).start()
 
-        w_a, w_b, f_b, w_z = {}, {}, {}, {}
+        w_a, w_b, f_b, w_z, rest = {}, {}, {}, {}, {}
 
         def a_send(k):
             hh = (h, 1 - h)[k]
@@ -360,8 +356,10 @@
                 w_a[k, d] = pass_on(unit(hh), da(d))
 
         def b_send(a, k, hh):
+            if k == 0:
+                rest[a] = ids()
             for d in (1, -1):
-                w_b[a, k, d] = pass_on(unit(hh, a), db(d))
+                w_b[a, k, d] = pass_on(unit(hh, a), db(d), None if d == (1, -1)[k] else rest[a])
 
         def first():
             for s in range(p * PARTS, (p + 1) * PARTS):
@@ -387,16 +385,18 @@
             d = (1, -1)[k]
             w_b[a, k, d].wait_recv()
             ref = unit((h, 1 - h)[k], a, -d)
-            f_b[a, d] = pass_on(ref, db(d))
+            if k == 0:
+                f_b[a] = ids()
+            pass_on(ref, db(d), f_b[a])
             if k == 1:
-                w_b[a, 0, -1].wait_recv()
+                two = unit(both, a, 1)
+                rcopy(WEIGHTS, two, two, rest[a], db(1)).wait_recv()
                 to_side(both, a, 1)
-                w_b[a, 1, 1].wait_recv()
                 to_side(both, a, -1)
 
         def finish(a):
-            f_b[a, 1].wait_recv()
-            f_b[a, -1].wait_recv()
+            two = unit(both, a, 2)
+            rcopy(WEIGHTS, two, two, f_b[a], db(1)).wait_recv()
             to_side(both, a, 2)
 
         P_ = functools.partial
@@ -470,7 +470,7 @@
     )(*arrays)
 
 
-N_SEM = 191
+N_SEM = 195
 VMEM_GRANT = 36 * 2**20
 
 

time: 133 us -> 131 us (0.985)
  Pallas kernels: 127 us -> 125 us
    pallas_call x1, Pallas kernels: 123 us -> 121 us  [on_device(): pl.pallas_call(kernel, out_shape=(f32, f32, f32, jax.ShapeDtypeStruct((4,...]
where the time goes in v5:
time: 131 us; the launch traced here: 130 us
  Pallas kernels  125 us (95%)
  local copies, waits for them, and re-layouts  5.29 us (4%)
    pallas_call x1, Pallas kernels, on_device(): pl.pallas_call(kernel, out_shape=(f32, f32, f32, jax.ShapeDtypeStruct((4,...  121 us
    unnamed x10, local copies, waits for them, and re-layouts  5.29 us
    pallas_call x1, Pallas kernels, write_out(): pl.pallas_call(copy_kernel, out_shape=[jax.ShapeDtypeStruct(a.shape, a.dt...  3.66 us

profile of v5, /device:TPU:1, one launch (start us, length us, event | category | flops | bytes accessed | tf_op | source)
XLA Modules:
  0.0 130.5 jit_solution(17178142656341582907)
XLA Ops:
  0.6 0.0 copy-start
  0.6 1.2 copy-done
  1.9 0.0 copy-start.1
  1.9 1.2 copy-done.1
  3.1 0.0 copy-start.2
  3.1 0.9 copy-done.2
  4.0 0.0 copy-start.3
  4.0 0.9 copy-done.3
  5.0 0.0 copy-start.4
  5.0 0.9 copy-done.4
  5.9 120.9 %shard_map.84 = (f32[64,1024]{1,0:T(8,128)S(1)}, f32[64,1024]{1,0:T(8,128)S(1)}, f32[64,1024]{1,0:T(8,128)S(1)}, bf16[4,2,4,2,64,1024]{5,4,3,2,1,0:T(8,128)(2,1)S(1)}) custom-call(bf16[128,4096]{1,0:T(8,128)(2,1)S(1)} %copy-done, bf16[128,4096]{1,0:T(8,128)(2,1)S(1)} %copy-done.1, f32[64,1024]{1,0:T(8,128)S(1)} %copy-done.2, f32[64,1024]{1,0:T(8,128)S(1)} %copy-done.3, ...), custom_call_target="tpu_custom_call" | custom-call | tf_op jit(solution)/shard_map/pallas_call | solution.py:480
  126.8 3.7 %shard_map.85 = (f32[64,1024]{1,0:T(8,128)}, f32[64,1024]{1,0:T(8,128)}, f32[64,1024]{1,0:T(8,128)}, bf16[4096,1024]{1,0:T(8,128)(2,1)}) custom-call(f32[64,1024]{1,0:T(8,128)S(1)} %get-tuple-element.8.refs_0_, f32[64,1024]{1,0:T(8,128)S(1)} %get-tuple-element.9.refs_1_, f32[64,1024]{1,0:T(8,128)S(1)} %get-tuple-element.10.refs_2_, ...), custom_call_target="tpu_custom_call" | custom-call | tf_op jit(solution)/shard_map/pallas_call | solution.py:463
Async XLA Ops:
  0.6 1.2 copy-start
  1.9 1.2 copy-start.1
  3.1 0.9 copy-start.2
  4.0 0.9 copy-start.3
  5.0 0.9 copy-start.4

commit v6 on v5

--- a/solution.py
+++ b/solution.py
@@ -28,7 +28,7 @@
     (14, 24, 25, 27, 31, 35, 38, 41, 42, 44, 45, 49),
 )
 CHAIN = (33, 52, 57.6, 63.2)
-STEP, HOP = 0.7, 5.2
+STEP, HOP = 0.7, 6.0
 TIMES = (6.0, 14.0, 11.0, 20.0, 16.0, 25.0, 31.0, 1.0)
 
 

time: 131 us -> 131 us (level)
  no operation moved by 1% of the time
where the time goes in v6:
time: 131 us
  Pallas kernels  125 us (95%)
  local copies, waits for them, and re-layouts  5.29 us (4%)
    pallas_call x1, Pallas kernels, on_device(): pl.pallas_call(kernel, out_shape=(f32, f32, f32, jax.ShapeDtypeStruct((4,...  121 us
    unnamed x10, local copies, waits for them, and re-layouts  5.29 us
    pallas_call x1, Pallas kernels, write_out(): pl.pallas_call(copy_kernel, out_shape=[jax.ShapeDtypeStruct(a.shape, a.dt...  3.66 us

profile of v6, /device:TPU:1, one launch (start us, length us, event | category | flops | bytes accessed | tf_op | source)
XLA Modules:
  0.0 131.0 jit_solution(15210885166515898652)
XLA Ops:
  0.6 0.0 copy-start
  0.6 1.2 copy-done
  1.9 0.0 copy-start.1
  1.9 1.2 copy-done.1
  3.1 0.0 copy-start.2
  3.1 0.9 copy-done.2
  4.0 0.0 copy-start.3
  4.0 0.9 copy-done.3
  5.0 0.0 copy-start.4
  5.0 0.9 copy-done.4
  5.9 121.4 %shard_map.84 = (f32[64,1024]{1,0:T(8,128)S(1)}, f32[64,1024]{1,0:T(8,128)S(1)}, f32[64,1024]{1,0:T(8,128)S(1)}, bf16[4,2,4,2,64,1024]{5,4,3,2,1,0:T(8,128)(2,1)S(1)}) custom-call(bf16[128,4096]{1,0:T(8,128)(2,1)S(1)} %copy-done, bf16[128,4096]{1,0:T(8,128)(2,1)S(1)} %copy-done.1, f32[64,1024]{1,0:T(8,128)S(1)} %copy-done.2, f32[64,1024]{1,0:T(8,128)S(1)} %copy-done.3, ...), custom_call_target="tpu_custom_call" | custom-call | tf_op jit(solution)/shard_map/pallas_call | solution.py:480
  127.3 3.7 %shard_map.85 = (f32[64,1024]{1,0:T(8,128)}, f32[64,1024]{1,0:T(8,128)}, f32[64,1024]{1,0:T(8,128)}, bf16[4096,1024]{1,0:T(8,128)(2,1)}) custom-call(f32[64,1024]{1,0:T(8,128)S(1)} %get-tuple-element.8.refs_0_, f32[64,1024]{1,0:T(8,128)S(1)} %get-tuple-element.9.refs_1_, f32[64,1024]{1,0:T(8,128)S(1)} %get-tuple-element.10.refs_2_, ...), custom_call_target="tpu_custom_call" | custom-call | tf_op jit(solution)/shard_map/pallas_call | solution.py:463
Async XLA Ops:
  0.6 1.2 copy-start
  1.9 1.2 copy-start.1
  3.1 0.9 copy-start.2
  4.0 0.9 copy-start.3
  5.0 0.9 copy-start.4
